TPU v7x, 32 devices: a whole 2x2x4 slice. The times are simulated.
32 devices in a mesh: seq: 4 (over z), dp: 8 (over y, x, core).
Axes of the slice: x: 2, y: 2, z: 4, core: 2. Of those that a mesh axis runs over, the one named last changes fastest.
Arguments:
- tokens: bfloat16 [8, 1024, 768], P('dp', 'seq'), may hold values from -6 to 6
- qkv_weight: bfloat16 [768, 2304], P('dp'), may hold values from -0.21875 to 0.21875
- proj_weight: bfloat16 [768, 768], P('dp'), may hold values from -0.875 to 0.875
- hidden_weight: bfloat16 [768, 3072], P('dp'), may hold values from -0.21875 to 0.21875
- output_weight: bfloat16 [3072, 768], P('dp'), may hold values from -0.109375 to 0.109375
- first_gain: bfloat16 [768], P('dp'), may hold values from 0.25 to 1.75
- first_bias: bfloat16 [768], P('dp'), may hold values from -2.5 to 2.5
- second_gain: bfloat16 [768], P('dp'), may hold values from 0.25 to 1.75
- second_bias: bfloat16 [768], P('dp'), may hold values from -2.5 to 2.5
- cotangent: bfloat16 [8, 1024, 768], P('dp', 'seq'), may hold values from -6 to 6
Outputs:
- block_out: bfloat16 [8, 1024, 768], P('dp', 'seq')
- tokens_gradient: bfloat16 [8, 1024, 768], P('dp', 'seq')
- qkv_gradient: float32 [768, 2304], P('dp')
- proj_gradient: float32 [768, 768], P('dp')
- hidden_gradient: float32 [768, 3072], P('dp')
- output_gradient: float32 [3072, 768], P('dp')
- first_gain_gradient: float32 [768], P('dp')
- first_bias_gradient: float32 [768], P('dp')
- second_gain_gradient: float32 [768], P('dp')
- second_bias_gradient: float32 [768], P('dp')
All inputs are finite; a program needn't handle non-finite values.
Results may differ from a plain program's by a relative error of at most 0.012.
Values may be sent and summed in bfloat16 or wider, within the bound.
A program may use at most 256 MiB of HBM per device.

v0:
```python
import jax
import jax.numpy as jnp
from jax import lax
from jax.sharding import PartitionSpec as P

HEAD_DIM = 64


def layer_norm(values, gain, bias):
    average = jnp.mean(values, -1, keepdims=True)
    centred = values - average
    variance = jnp.mean(centred * centred, -1, keepdims=True)
    return centred * lax.rsqrt(variance + 1e-05) * gain + bias


def gelu_tanh(values):
    return jax.nn.gelu(values, approximate=True)


def matmul(left, right):
    return jnp.dot(left, right, preferred_element_type=jnp.float32)


def matmul_left_t(left, right):
    return lax.dot_general(
        left, right, (((0,), (0,)), ((), ())), preferred_element_type=jnp.float32
    )


def matmul_right_t(left, right):
    return lax.dot_general(
        left, right, (((1,), (1,)), ((), ())), preferred_element_type=jnp.float32
    )


def term_block(pairs, row_start, row_count, column_block, parts):
    pieces = []
    for left, right in pairs:
        width = right.shape[1] // parts
        left_rows = lax.dynamic_slice_in_dim(left, row_start, row_count, 1)
        right_cols = lax.dynamic_slice_in_dim(right, column_block * width, width, 1)
        pieces.append(matmul_left_t(left_rows, right_cols))
    return jnp.concatenate(pieces, axis=1)


def on_device(
    tokens,
    qkv_weight,
    proj_weight,
    hidden_weight,
    output_weight,
    first_gain,
    first_bias,
    second_gain,
    second_bias,
    cotangent,
):
    gathered = (
        lax.all_gather(qkv_weight, "dp", axis=0, tiled=True),
        lax.all_gather(proj_weight, "dp", axis=0, tiled=True),
        lax.all_gather(hidden_weight, "dp", axis=0, tiled=True),
        lax.all_gather(output_weight, "dp", axis=0, tiled=True),
        lax.all_gather(first_gain, "dp", axis=0, tiled=True),
        lax.all_gather(first_bias, "dp", axis=0, tiled=True),
        lax.all_gather(second_gain, "dp", axis=0, tiled=True),
        lax.all_gather(second_bias, "dp", axis=0, tiled=True),
    )
    wide_qkv, wide_proj, wide_hidden, wide_output, gain_one, bias_one, gain_two, bias_two = gathered
    inputs = tokens[0].astype(jnp.float32)
    width = inputs.shape[1]
    normed_one, norm_pull_one = jax.vjp(
        layer_norm, inputs, gain_one.astype(jnp.float32), bias_one.astype(jnp.float32)
    )
    lowered_one = normed_one.astype(jnp.bfloat16)
    projected = matmul(lowered_one, wide_qkv)
    queries = projected[:, :width].astype(jnp.bfloat16)
    keys = projected[:, width : 2 * width].astype(jnp.bfloat16)
    values = projected[:, 2 * width :].astype(jnp.bfloat16)
    head_queries, head_keys, head_values = (
        lax.all_to_all(queries, "seq", split_axis=1, concat_axis=0, tiled=True),
        lax.all_to_all(keys, "seq", split_axis=1, concat_axis=0, tiled=True),
        lax.all_to_all(values, "seq", split_axis=1, concat_axis=0, tiled=True),
    )
    length = head_queries.shape[0]
    local_width = head_queries.shape[1]
    heads_here = local_width // HEAD_DIM
    block_rows = min(512, length)
    blocks = length // block_rows
    scale = HEAD_DIM ** (-0.5)
    keys_split = head_keys.reshape(length, heads_here, HEAD_DIM)
    values_split = head_values.reshape(length, heads_here, HEAD_DIM)
    queries_split = head_queries.reshape(blocks, block_rows, heads_here, HEAD_DIM)
    starts = jnp.arange(blocks) * block_rows
    key_index = jnp.arange(length)

    def scores_of(query_block, first_row):
        raw = jnp.einsum(
            "qhd,khd->hqk", query_block, keys_split, preferred_element_type=jnp.float32
        )
        positions = first_row + jnp.arange(block_rows)
        causal = key_index[None, :] <= positions[:, None]
        return jnp.where(causal[None], raw * scale, -1e30)

    def forward_block(carry, pair):
        query_block, first_row = pair
        scores = scores_of(query_block, first_row)
        largest = jnp.max(scores, -1, keepdims=True)
        expo = jnp.exp(scores - largest)
        total = jnp.sum(expo, -1, keepdims=True)
        probs = (expo / total).astype(jnp.bfloat16)
        context = jnp.einsum(
            "hqk,khd->qhd", probs, values_split, preferred_element_type=jnp.float32
        )
        return (
            carry,
            (
                context.astype(jnp.bfloat16).reshape(block_rows, local_width),
                (largest + jnp.log(total))[..., 0],
            ),
        )

    _, (context_blocks, log_totals) = lax.scan(
        forward_block, jnp.zeros((), jnp.float32), (queries_split, starts)
    )
    context_heads = context_blocks.reshape(length, local_width)
    context = lax.all_to_all(context_heads, "seq", split_axis=0, concat_axis=1, tiled=True)
    middle = inputs + matmul(context, wide_proj)
    normed_two, norm_pull_two = jax.vjp(
        layer_norm, middle, gain_two.astype(jnp.float32), bias_two.astype(jnp.float32)
    )
    lowered_two = normed_two.astype(jnp.bfloat16)
    hidden_pre = matmul(lowered_two, wide_hidden)
    activated_float, gelu_pull = jax.vjp(gelu_tanh, hidden_pre)
    activated = activated_float.astype(jnp.bfloat16)
    block_out = middle + matmul(activated, wide_output)
    back_qkv, back_proj, back_hidden, back_output = (wide_qkv, wide_proj, wide_hidden, wide_output)
    out_grad = cotangent[0]
    act_grad = matmul_right_t(out_grad, back_output)
    pre_grad = gelu_pull(act_grad)[0].astype(jnp.bfloat16)
    normed_two_grad = matmul_right_t(pre_grad, back_hidden)
    middle_part, gain_two_term, bias_two_term = norm_pull_two(normed_two_grad)
    middle_grad = out_grad.astype(jnp.float32) + middle_part
    attn_grad = middle_grad.astype(jnp.bfloat16)
    context_grad = matmul_right_t(attn_grad, back_proj).astype(jnp.bfloat16)
    grad_heads = lax.all_to_all(context_grad, "seq", split_axis=1, concat_axis=0, tiled=True)
    grad_split = grad_heads.reshape(blocks, block_rows, heads_here, HEAD_DIM)

    def backward_block(carry, quad):
        key_sum, value_sum = carry
        query_block, grad_block, log_block, first_row = quad
        scores = scores_of(query_block, first_row)
        probs = jnp.exp(scores - log_block[..., None])
        low_probs = probs.astype(jnp.bfloat16)
        value_sum = value_sum + jnp.einsum(
            "hqk,qhd->khd", low_probs, grad_block, preferred_element_type=jnp.float32
        )
        prob_grad = jnp.einsum(
            "qhd,khd->hqk", grad_block, values_split, preferred_element_type=jnp.float32
        )
        score_grad = (probs * (prob_grad - jnp.sum(probs * prob_grad, -1, keepdims=True))).astype(
            jnp.bfloat16
        )
        query_grad = (
            jnp.einsum("hqk,khd->qhd", score_grad, keys_split, preferred_element_type=jnp.float32)
            * scale
        )
        key_sum = (
            key_sum
            + jnp.einsum(
                "hqk,qhd->khd", score_grad, query_block, preferred_element_type=jnp.float32
            )
            * scale
        )
        return (
            (key_sum, value_sum),
            query_grad.astype(jnp.bfloat16).reshape(block_rows, local_width),
        )

    empty = jnp.zeros((length, heads_here, HEAD_DIM), jnp.float32)
    (key_sum, value_sum), query_blocks = lax.scan(
        backward_block, (empty, empty), (queries_split, grad_split, log_totals, starts)
    )
    query_grads = query_blocks.reshape(length, local_width)
    key_grads = key_sum.astype(jnp.bfloat16).reshape(length, local_width)
    value_grads = value_sum.astype(jnp.bfloat16).reshape(length, local_width)
    token_query, token_key, token_value = (
        lax.all_to_all(query_grads, "seq", split_axis=0, concat_axis=1, tiled=True),
        lax.all_to_all(key_grads, "seq", split_axis=0, concat_axis=1, tiled=True),
        lax.all_to_all(value_grads, "seq", split_axis=0, concat_axis=1, tiled=True),
    )
    qkv_grad = jnp.concatenate([token_query, token_key, token_value], axis=1)
    normed_one_grad = matmul_right_t(qkv_grad, back_qkv)
    input_part, gain_one_term, bias_one_term = norm_pull_one(normed_one_grad)
    tokens_gradient = (middle_grad + input_part).astype(jnp.bfloat16)
    groups = lax.axis_size("dp")
    parts = lax.axis_size("seq")
    model_rows = width // groups
    hidden_rows = activated.shape[1] // groups
    width_pairs = ((lowered_one, qkv_grad), (context, attn_grad), (lowered_two, pre_grad))
    hidden_pairs = ((activated, out_grad),)
    start = jnp.int32(0)
    pieces = []
    for offset in range(model_rows * lax.axis_size(("seq", "dp")) // model_rows):
        index = start // model_rows + offset
        pieces.append(
            term_block(width_pairs, index % groups * model_rows, model_rows, index // groups, parts)
        )
    width_block = lax.psum_scatter(
        jnp.concatenate(pieces, axis=0), ("seq", "dp"), scatter_dimension=0, tiled=True
    )
    start = jnp.int32(0)
    pieces = []
    for offset in range(hidden_rows * lax.axis_size(("seq", "dp")) // hidden_rows):
        index = start // hidden_rows + offset
        pieces.append(
            term_block(
                hidden_pairs, index % groups * hidden_rows, hidden_rows, index // groups, parts
            )
        )
    hidden_block = lax.psum_scatter(
        jnp.concatenate(pieces, axis=0), ("seq", "dp"), scatter_dimension=0, tiled=True
    )
    width_full, hidden_full = (
        lax.all_gather(width_block.astype(jnp.bfloat16), "seq", axis=1, tiled=True).astype(
            width_block.dtype
        ),
        lax.all_gather(hidden_block.astype(jnp.bfloat16), "seq", axis=1, tiled=True).astype(
            hidden_block.dtype
        ),
    )
    arranged = width_full.reshape(model_rows, parts, width_full.shape[1] // parts)
    qkv_cols = 3 * width // parts
    proj_cols = width // parts
    qkv_gradient = arranged[:, :, :qkv_cols].reshape(model_rows, 3 * width)
    proj_gradient = arranged[:, :, qkv_cols : qkv_cols + proj_cols].reshape(model_rows, width)
    hidden_gradient = arranged[:, :, qkv_cols + proj_cols :].reshape(
        model_rows, parts * (arranged.shape[2] - qkv_cols - proj_cols)
    )
    norm_shares = (
        lax.psum_scatter(gain_one_term, "dp", scatter_dimension=0, tiled=True),
        lax.psum_scatter(bias_one_term, "dp", scatter_dimension=0, tiled=True),
        lax.psum_scatter(gain_two_term, "dp", scatter_dimension=0, tiled=True),
        lax.psum_scatter(bias_two_term, "dp", scatter_dimension=0, tiled=True),
    )
    norm_grads = lax.psum((norm_shares[0], norm_shares[1], norm_shares[2], norm_shares[3]), "seq")
    return (
        block_out.astype(jnp.bfloat16)[None],
        tokens_gradient[None],
        qkv_gradient,
        proj_gradient,
        hidden_gradient,
        hidden_full,
        norm_grads[0],
        norm_grads[1],
        norm_grads[2],
        norm_grads[3],
    )


def solution(mesh):
    placed = (
        P("dp", "seq", None),
        P("dp", None),
        P("dp", None),
        P("dp", None),
        P("dp", None),
        P("dp"),
        P("dp"),
        P("dp"),
        P("dp"),
        P("dp", "seq", None),
    )
    return jax.shard_map(
        on_device,
        mesh=mesh,
        in_specs=placed,
        out_specs=(
            P("dp", "seq", None),
            P("dp", "seq", None),
            P("dp", None),
            P("dp", None),
            P("dp", None),
            P("dp", None),
            P("dp"),
            P("dp"),
            P("dp"),
            P("dp"),
        ),
        check_vma=False,
    )
```

profile of v0, /device:TPU:0, one launch (start us, length us, event | category | flops | bytes accessed | tf_op | source)
XLA Modules:
  0.0 806.0 jit_solution(17578302186303691256)
XLA Ops:
  14.7 15.5 %all-reduce.10 = (bf16[768]{0:T(1024)(128)(2,1)S(1)}, bf16[768]{0:T(1024)(128)(2,1)S(1)}, bf16[768]{0:T(1024)(128)(2,1)S(1)}, bf16[768]{0:T(1024)(128)(2,1)S(1)}) all-reduce(bf16[768]{0:T(1024)(128)(2,1)S(1)} %dynamic-update-slice.1, bf16[768]{0:T(1024)(128)(2,1)S(1)} %dynamic-update-slice, ...), channel_id=1, replica_groups=mesh['seq'=4,'dp'=8] {'dp'}, use_global_device_ids=true, to_apply=%add.1 | all-reduce | flops 3072 | bytes 12288
  35.1 11.7 %all-gather.6.cloned.1.call-done = bf16[768,2304]{1,0:T(8,128)(2,1)} async-done(((bf16[96,2304]{1,0:T(8,128)(2,1)}), bf16[768,2304]{1,0:T(8,128)(2,1)}) %all-gather.6.cloned.1.call-update) | async-done | bytes 3538960 | tf_op jit(solution)/shard_map/all_gather | solution.py:59
  46.8 3.1 convolution_convert_fusion
  50.9 4.6 all-to-all-start
  56.4 11.2 %all-to-all-done = bf16[256,4,192]{0,2,1:T(8,128)(2,1)S(1)} async-done(((bf16[256,4,192]{0,2,1:T(8,128)(2,1)}), bf16[256,4,192]{0,2,1:T(8,128)(2,1)S(1)}, u32[]{:S(2)}, u32[]{:S(2)}) %all-to-all-start) | async-done | bytes 393248 | tf_op jit(solution)/shard_map/all_to_all | solution.py:80
  67.6 3.5 all-to-all-start.1
  72.0 10.3 %all-to-all-done.1 = bf16[256,4,192]{0,2,1:T(8,128)(2,1)S(1)} async-done(((bf16[256,4,192]{0,2,1:T(8,128)(2,1)}), bf16[256,4,192]{0,2,1:T(8,128)(2,1)S(1)}, u32[]{:S(2)}, u32[]{:S(2)}) %all-to-all-start.1) | async-done | bytes 393248 | tf_op jit(solution)/shard_map/all_to_all | solution.py:81
  82.3 3.5 all-to-all-start.2
  88.3 7.3 all-to-all-done.2
  96.9 18.0 %while.28 = (s32[]{:T(128)}, bf16[2,512,192]{1,2,0:T(8,128)(2,1)S(1)}, f32[2,3,512]{2,1,0:T(4,128)S(1)}, s32[2]{0:T(128)S(1)}, bf16[2,512,3,64]{1,3,2,0:T(8,128)...) while((s32[]{:T(128)}, ...), condition=%wide.region_5.6_spmd.clone, body=%wide.region_2.5_spmd.clone.sunk | while | flops 422149120 | bytes 22603896 | solution.py:122
  98.6 2.3 fusion.510
  102.7 3.2 fusion.512
  107.6 2.3 fusion.510
  111.7 3.2 fusion.512
  116.3 3.9 all-to-all-start.3
  120.4 9.7 %all-to-all-done.3 = bf16[4,256,192]{1,2,0:T(8,128)(2,1)S(1)} async-done(((bf16[4,256,192]{1,2,0:T(8,128)(2,1)}), bf16[4,256,192]{1,2,0:T(8,128)(2,1)S(1)}, u32[]{:S(2)}, u32[]{:S(2)}) %all-to-all-start.3) | async-done | bytes 393248 | tf_op jit(solution)/shard_map/all_to_all | solution.py:126
  130.0 2.0 fusion.452
  132.5 6.8 multiply_convert_fusion.1
  139.3 15.0 %all-gather.12.cloned.1.call-done = bf16[3072,768]{1,0:T(8,128)(2,1)} async-done(((bf16[384,768]{1,0:T(8,128)(2,1)}), bf16[3072,768]{1,0:T(8,128)(2,1)}) %all-gather.12.cloned.1.call-update) | async-done | bytes 4718608 | tf_op jit(solution)/shard_map/all_gather | solution.py:62
  154.3 6.7 fusion.49
  162.2 2.2 multiply_reduce_fusion.1
  218.4 4.8 all-to-all-start.4
  226.0 9.3 %all-to-all-done.4 = bf16[256,4,192]{0,2,1:T(8,128)(2,1)S(1)} async-done(((bf16[256,4,192]{0,2,1:T(8,128)(2,1)}), bf16[256,4,192]{0,2,1:T(8,128)(2,1)S(1)}, u32[]{:S(2)}, u32[]{:S(2)}) %all-to-all-start.4) | async-done | bytes 393248 | tf_op jit(solution)/shard_map/all_to_all | solution.py:145
  237.4 37.9 %while.29 = (s32[]{:T(128)}, f32[1024,3,64]{0,2,1:T(8,128)}, f32[1024,3,64]{0,2,1:T(8,128)}, bf16[2,512,192]{1,2,0:T(8,128)(2,1)}, bf16[2,512,3,64]{1,3,2,0:T(8,...) while((s32[]{:T(128)}, f32[1024,3,64]{0,2,1:T(8,128)}, ...), condition=%wide.region_12.13_spmd.clone, body=%wide.region_10.12_spmd.clone.sunk | while | flops 1031928832 | bytes 110655824 | solution.py:180
  237.4 2.0 fusion.522
  241.2 4.1 multiply_reduce_fusion.5
  247.1 2.6 fusion.523
  250.3 4.0 fusion.524
  260.0 4.1 multiply_reduce_fusion.5
  265.9 2.9 fusion.523
  269.2 4.3 fusion.524
  277.8 3.5 all-to-all-start.5
  283.0 2.1 fusion.142
  285.2 2.1 fusion.140
  292.5 3.5 all-to-all-start.7
  300.8 5.6 all-to-all-done.7
  306.4 3.5 all-to-all-start.6
  313.1 6.6 all-to-all-done.6
  443.1 169.7 %reduce-scatter.3.cloned.1.call-done = f32[96,1536]{1,0:T(8,128)} async-done(((f32[3072,1536]{1,0:T(8,128)}), f32[96,1536]{1,0:T(8,128)}) %reduce-scatter.3.cloned.1.call-update) | async-done | bytes 589840 | tf_op jit(solution)/shard_map/reduce_scatter | solution.py:208
  614.6 4.8 fusion.51
  621.8 22.9 %all-reduce.8 = (f32[768]{0:T(1024)S(1)}, f32[768]{0:T(1024)S(1)}, f32[768]{0:T(1024)S(1)}, f32[768]{0:T(1024)S(1)}) all-reduce(f32[768]{0:T(1024)S(1)} %get-tuple-element.261, f32[768]{0:T(1024)} %get-tuple-element.264, f32[768]{0:T(1024)} %get-tuple-element.259, ...), channel_id=4, replica_groups=mesh['seq'=4,'dp'=8] {'dp'}, use_global_device_ids=true, to_apply=%region_18.19.clone | all-reduce | flops 3072 | bytes 24576
  645.0 10.7 %all-reduce.9 = (f32[96]{0:T(128)}, f32[96]{0:T(128)}, f32[96]{0:T(128)}, f32[96]{0:T(128)}) all-reduce(f32[96]{0:T(128)S(1)} %dynamic-slice.37, f32[96]{0:T(128)S(1)} %dynamic-slice.39, f32[96]{0:T(128)S(1)} %dynamic-slice.41, f32[96]{0:T(128)S(1)} %dynamic-slice.43), channel_id=1, replica_groups=mesh['seq'=4,'dp'=8] {'seq'}, use_global_device_ids=true, to_apply=%region_19.20 | all-reduce | flops 384 | bytes 3072 | tf_op jit(solution)/shard_map/psum | solution.py:245
  656.8 96.3 %reduce-scatter.5.cloned.1.call-done = f32[384,192]{0,1:T(8,128)} async-done(((f32[12288,192]{0,1:T(8,128)}), f32[384,192]{0,1:T(8,128)}) %reduce-scatter.5.cloned.1.call-update) | async-done | bytes 294928 | tf_op jit(solution)/shard_map/reduce_scatter | solution.py:220
  754.1 18.9 %all_gather.39 = bf16[384,768]{0,1:T(8,128)(2,1)S(1)} all-gather(bf16[384,192]{0,1:T(8,128)(2,1)S(1)} %convert_element_type.103), channel_id=1, replica_groups=mesh['seq'=4,'dp'=8] {'seq'}, dimensions={1}, use_global_device_ids=true | all-gather | bytes 737280 | tf_op jit(solution)/shard_map/all_gather | solution.py:227
  774.3 12.9 %all-gather.14.cloned.1.call-done = bf16[96,6144]{1,0:T(8,128)(2,1)} async-done(((bf16[96,1536]{1,0:T(8,128)(2,1)}), bf16[96,6144]{1,0:T(8,128)(2,1)}) %all-gather.14.cloned.1.call-update) | async-done | bytes 1179664 | tf_op jit(solution)/shard_map/all_gather | solution.py:224
  787.2 3.0 reshape.284
  792.6 2.7 reshape.280
  796.2 2.5 copy.73
  (479 shorter events, 252.0 us)
Async XLA Ops:
  7.2 39.6 %all-gather.6.cloned.1.call-start = ((), (), s32[]{:S(2)}) async-start(), calls=%async_computation.10 | async-start | bytes 3981312 | tf_op jit(solution)/shard_map/all_gather | solution.py:59
  7.9 112.4 %all-gather.8.cloned.1.call-start = ((), (), s32[]{:S(2)}) async-start(), calls=%async_computation.11 | async-start | bytes 1327104 | tf_op jit(solution)/shard_map/all_gather | solution.py:60
  8.7 123.9 %all-gather.10.cloned.1.call-start = ((), (), s32[]{:S(2)}) async-start(), calls=%async_computation.12 | async-start | bytes 5308416 | tf_op jit(solution)/shard_map/all_gather | solution.py:61
  35.1 47.2 %copy-start.9 = (bf16[256,768]{1,0:T(8,128)(2,1)}, bf16[256,768]{1,0:T(8,128)(2,1)S(1)}, u32[]{:S(2)}) copy-start(bf16[256,768]{1,0:T(8,128)(2,1)S(1)} %fusion.66) | copy-start | bytes 1179652
  50.9 16.7 %all-to-all-start = ((bf16[256,4,192]{0,2,1:T(8,128)(2,1)}), bf16[256,4,192]{0,2,1:T(8,128)(2,1)S(1)}, u32[]{:S(2)}, u32[]{:S(2)}) async-start(bf16[256,4,192]{0,2,1:T(8,128)(2,1)} %bitcast.2), calls=%async_computation | async-start | bytes 786432 | tf_op jit(solution)/shard_map/all_to_all | solution.py:80
  67.6 14.7 %all-to-all-start.1 = ((bf16[256,4,192]{0,2,1:T(8,128)(2,1)}), bf16[256,4,192]{0,2,1:T(8,128)(2,1)S(1)}, u32[]{:S(2)}, u32[]{:S(2)}) async-start(bf16[256,4,192]{0,2,1:T(8,128)(2,1)} %bitcast.4), calls=%async_computation.1 | async-start | bytes 786432 | tf_op jit(solution)/shard_map/all_to_all | solution.py:81
  82.3 13.3 %all-to-all-start.2 = ((bf16[256,4,192]{0,2,1:T(8,128)(2,1)}), bf16[256,4,192]{0,2,1:T(8,128)(2,1)S(1)}, u32[]{:S(2)}, u32[]{:S(2)}) async-start(bf16[256,4,192]{0,2,1:T(8,128)(2,1)} %bitcast.6), calls=%async_computation.2 | async-start | bytes 786432 | tf_op jit(solution)/shard_map/all_to_all | solution.py:82
  85.8 68.6 %all-gather.12.cloned.1.call-start = ((), (), s32[]{:S(2)}) async-start(), calls=%async_computation.13 | async-start | bytes 5308416 | tf_op jit(solution)/shard_map/all_gather | solution.py:62
  96.9 33.1 %copy-start.12 = (bf16[1,256,768]{2,1,0:T(8,128)(2,1)S(1)}, bf16[1,256,768]{2,1,0:T(8,128)(2,1)}, u32[]{:S(2)}) copy-start(bf16[1,256,768]{2,1,0:T(8,128)(2,1)} %param.14) | copy-start | bytes 1179652
  115.0 24.4 %copy-start.66 = (f32[2,3,512]{2,1,0:T(4,128)}, f32[2,3,512]{2,1,0:T(4,128)S(1)}, u32[]{:S(2)}) copy-start(f32[2,3,512]{2,1,0:T(4,128)S(1)} %get-tuple-element.474) | copy-start | bytes 36868
  116.3 13.7 %all-to-all-start.3 = ((bf16[4,256,192]{1,2,0:T(8,128)(2,1)}), bf16[4,256,192]{1,2,0:T(8,128)(2,1)S(1)}, u32[]{:S(2)}, u32[]{:S(2)}) async-start(bf16[4,256,192]{1,2,0:T(8,128)(2,1)} %copy.63), calls=%async_computation.3 | async-start | bytes 786432 | tf_op jit(solution)/shard_map/all_to_all | solution.py:126
  130.0 93.2 %copy-start.14 = (bf16[4,256,192]{1,2,0:T(8,128)(2,1)}, bf16[4,256,192]{1,2,0:T(8,128)(2,1)S(1)}, u32[]{:S(2)}) copy-start(bf16[4,256,192]{1,2,0:T(8,128)(2,1)S(1)} %all-to-all-done.3) | copy-start | bytes 1179652
  132.5 92.5 %copy-start.11 = (bf16[256,768]{1,0:T(8,128)(2,1)}, bf16[256,768]{1,0:T(8,128)(2,1)S(1)}, u32[]{:S(2)}) copy-start(bf16[256,768]{1,0:T(8,128)(2,1)S(1)} %add_convert_fusion.1) | copy-start | bytes 1179652
  132.5 21.8 %copy-start.4 = (bf16[1,256,768]{2,1,0:T(8,128)(2,1)S(1)}, bf16[1,256,768]{2,1,0:T(8,128)(2,1)}, u32[]{:S(2)}) copy-start(bf16[1,256,768]{2,1,0:T(8,128)(2,1)} %param.23) | copy-start | bytes 1179652
  161.1 63.9 %copy-start.3 = (bf16[256,3072]{1,0:T(8,128)(2,1)}, bf16[256,3072]{1,0:T(8,128)(2,1)S(1)}, u32[]{:S(2)}) copy-start(bf16[256,3072]{1,0:T(8,128)(2,1)S(1)} %fusion.49) | copy-start | bytes 4718596
  164.8 21.1 %copy-start.17 = (f32[256,768]{1,0:T(8,128)}, f32[256,768]{1,0:T(8,128)S(1)}, u32[]{:S(2)}) copy-start(f32[256,768]{1,0:T(8,128)S(1)} %get-tuple-element.313) | copy-start | bytes 2359300
  165.0 58.2 %copy-start.6 = (bf16[256,768]{1,0:T(8,128)(2,1)}, bf16[256,768]{1,0:T(8,128)(2,1)S(1)}, u32[]{:S(2)}) copy-start(bf16[256,768]{1,0:T(8,128)(2,1)S(1)} %fusion.70) | copy-start | bytes 1179652
  194.2 22.8 %copy-start.19 = (bf16[768,768]{1,0:T(8,128)(2,1)S(1)}, bf16[768,768]{1,0:T(8,128)(2,1)}, u32[]{:S(2)}) copy-start(bf16[768,768]{1,0:T(8,128)(2,1)} %all-gather.8.cloned.1.call-done) | copy-start | bytes 3538948
  218.4 16.9 %all-to-all-start.4 = ((bf16[256,4,192]{0,2,1:T(8,128)(2,1)}), bf16[256,4,192]{0,2,1:T(8,128)(2,1)S(1)}, u32[]{:S(2)}, u32[]{:S(2)}) async-start(bf16[256,4,192]{0,2,1:T(8,128)(2,1)} %bitcast.333), calls=%async_computation.4 | async-start | bytes 786432 | tf_op jit(solution)/shard_map/all_to_all | solution.py:145
  275.3 14.2 %copy-start.7 = (f32[1024,3,64]{0,2,1:T(8,128)S(1)}, f32[1024,3,64]{0,2,1:T(8,128)}, u32[]{:S(2)}) copy-start(f32[1024,3,64]{0,2,1:T(8,128)} %get-tuple-element.115) | copy-start | bytes 2359300
  275.3 20.6 %copy-start.10 = (bf16[256,768]{1,0:T(8,128)(2,1)S(1)}, bf16[256,768]{1,0:T(8,128)(2,1)}, u32[]{:S(2)}) copy-start(bf16[256,768]{1,0:T(8,128)(2,1)} %copy-done.9) | copy-start | bytes 1179652
  277.8 14.7 %all-to-all-start.5 = ((bf16[4,256,192]{1,2,0:T(8,128)(2,1)}), bf16[4,256,192]{1,2,0:T(8,128)(2,1)S(1)}, u32[]{:S(2)}, u32[]{:S(2)}) async-start(bf16[4,256,192]{1,2,0:T(8,128)(2,1)} %copy.69), calls=%async_computation.5 | async-start | bytes 786432 | tf_op jit(solution)/shard_map/all_to_all | solution.py:187
  292.5 13.9 %all-to-all-start.7 = ((bf16[4,256,192]{1,2,0:T(8,128)(2,1)}), bf16[4,256,192]{1,2,0:T(8,128)(2,1)S(1)}, u32[]{:S(2)}, u32[]{:S(2)}) async-start(bf16[4,256,192]{1,2,0:T(8,128)(2,1)} %copy.71), calls=%async_computation.7 | async-start | bytes 786432 | tf_op jit(solution)/shard_map/all_to_all | solution.py:189
  306.4 13.3 %all-to-all-start.6 = ((bf16[4,256,192]{1,2,0:T(8,128)(2,1)}), bf16[4,256,192]{1,2,0:T(8,128)(2,1)S(1)}, u32[]{:S(2)}, u32[]{:S(2)}) async-start(bf16[4,256,192]{1,2,0:T(8,128)(2,1)} %copy.70), calls=%async_computation.6 | async-start | bytes 786432 | tf_op jit(solution)/shard_map/all_to_all | solution.py:188
  309.8 303.0 %reduce-scatter.3.cloned.1.call-start = ((), (), s32[]{:S(2)}) async-start(), calls=%async_computation.14 | async-start | bytes 19464192 | tf_op jit(solution)/shard_map/reduce_scatter | solution.py:208
  322.7 20.8 %copy-start.44 = (f32[96,768]{1,0:T(8,128)S(1)}, f32[96,768]{1,0:T(8,128)}, u32[]{:S(2)}) copy-start(f32[96,768]{1,0:T(8,128)} %fusion.202) | copy-start | bytes 884740
  322.7 20.8 %copy-start.65 = (f32[96,192]{1,0:T(8,128)S(1)}, f32[96,192]{1,0:T(8,128)}, u32[]{:S(2)}) copy-start(f32[96,192]{1,0:T(8,128)} %fusion.378) | copy-start | bytes 221188
  326.6 18.9 %copy-start.64 = (f32[96,192]{1,0:T(8,128)S(1)}, f32[96,192]{1,0:T(8,128)}, u32[]{:S(2)}) copy-start(f32[96,192]{1,0:T(8,128)} %fusion.370) | copy-start | bytes 221188
  330.6 17.0 %copy-start.63 = (f32[96,192]{1,0:T(8,128)S(1)}, f32[96,192]{1,0:T(8,128)}, u32[]{:S(2)}) copy-start(f32[96,192]{1,0:T(8,128)} %fusion.362) | copy-start | bytes 221188
  335.5 14.1 %copy-start.45 = (f32[96,768]{1,0:T(8,128)S(1)}, f32[96,768]{1,0:T(8,128)}, u32[]{:S(2)}) copy-start(f32[96,768]{1,0:T(8,128)} %fusion.196) | copy-start | bytes 884740
  338.5 13.2 %copy-start.62 = (f32[96,192]{1,0:T(8,128)S(1)}, f32[96,192]{1,0:T(8,128)}, u32[]{:S(2)}) copy-start(f32[96,192]{1,0:T(8,128)} %fusion.346) | copy-start | bytes 221188
  342.4 11.3 %copy-start.43 = (f32[96,768]{1,0:T(8,128)S(1)}, f32[96,768]{1,0:T(8,128)}, u32[]{:S(2)}) copy-start(f32[96,768]{1,0:T(8,128)} %fusion.192) | copy-start | bytes 884740
  342.4 11.3 %copy-start.61 = (f32[96,192]{1,0:T(8,128)S(1)}, f32[96,192]{1,0:T(8,128)}, u32[]{:S(2)}) copy-start(f32[96,192]{1,0:T(8,128)} %fusion.338) | copy-start | bytes 221188
  345.4 10.3 %copy-start.60 = (f32[96,192]{1,0:T(8,128)S(1)}, f32[96,192]{1,0:T(8,128)}, u32[]{:S(2)}) copy-start(f32[96,192]{1,0:T(8,128)} %fusion.330) | copy-start | bytes 221188
  347.5 10.3 %copy-start.42 = (f32[96,768]{1,0:T(8,128)S(1)}, f32[96,768]{1,0:T(8,128)}, u32[]{:S(2)}) copy-start(f32[96,768]{1,0:T(8,128)} %fusion.188) | copy-start | bytes 884740
  349.6 10.3 %copy-start.40 = (f32[96,768]{1,0:T(8,128)S(1)}, f32[96,768]{1,0:T(8,128)}, u32[]{:S(2)}) copy-start(f32[96,768]{1,0:T(8,128)} %fusion.186) | copy-start | bytes 884740
  351.7 10.3 %copy-start.39 = (f32[96,768]{1,0:T(8,128)S(1)}, f32[96,768]{1,0:T(8,128)}, u32[]{:S(2)}) copy-start(f32[96,768]{1,0:T(8,128)} %fusion.184) | copy-start | bytes 884740
  362.0 10.3 %copy-start.35 = (f32[96,768]{1,0:T(8,128)S(1)}, f32[96,768]{1,0:T(8,128)}, u32[]{:S(2)}) copy-start(f32[96,768]{1,0:T(8,128)} %fusion.174) | copy-start | bytes 884740
  366.0 10.3 %copy-start.33 = (f32[96,768]{1,0:T(8,128)S(1)}, f32[96,768]{1,0:T(8,128)}, u32[]{:S(2)}) copy-start(f32[96,768]{1,0:T(8,128)} %fusion.170) | copy-start | bytes 884740
  366.0 10.3 %copy-start.55 = (f32[96,192]{1,0:T(8,128)S(1)}, f32[96,192]{1,0:T(8,128)}, u32[]{:S(2)}) copy-start(f32[96,192]{1,0:T(8,128)} %fusion.374) | copy-start | bytes 221188
  368.0 10.3 %copy-start.32 = (f32[96,768]{1,0:T(8,128)S(1)}, f32[96,768]{1,0:T(8,128)}, u32[]{:S(2)}) copy-start(f32[96,768]{1,0:T(8,128)} %fusion.168) | copy-start | bytes 884740
  368.0 10.3 %copy-start.54 = (f32[96,192]{1,0:T(8,128)S(1)}, f32[96,192]{1,0:T(8,128)}, u32[]{:S(2)}) copy-start(f32[96,192]{1,0:T(8,128)} %fusion.366) | copy-start | bytes 221188
  407.7 345.4 %reduce-scatter.5.cloned.1.call-start = ((), (), s32[]{:S(2)}) async-start(), calls=%async_computation.16 | async-start | bytes 9732096 | tf_op jit(solution)/shard_map/reduce_scatter | solution.py:220
  442.3 177.1 %copy-start.13 = (bf16[1,256,768]{2,1,0:T(8,128)(2,1)S(1)}, bf16[1,256,768]{2,1,0:T(8,128)(2,1)}, u32[]{:S(2)}) copy-start(bf16[1,256,768]{2,1,0:T(8,128)(2,1)} %param.14) | copy-start | bytes 1179652
  442.3 177.1 %copy-start.69 = (f32[768]{0:T(1024)S(1)}, f32[768]{0:T(1024)}, u32[]{:S(2)}) copy-start(f32[768]{0:T(1024)} %copy-done.68) | copy-start | bytes 9220
  442.4 177.1 %copy-start.71 = (f32[256]{0:T(256)S(1)}, f32[256]{0:T(256)}, u32[]{:S(2)}) copy-start(f32[256]{0:T(256)} %copy-done.70) | copy-start | bytes 3076
  442.4 344.8 %all-gather.14.cloned.1.call-start = ((), (), s32[]{:S(2)}) async-start(), calls=%async_computation.15 | async-start | bytes 1474560 | tf_op jit(solution)/shard_map/all_gather | solution.py:224
  619.5 36.2 %copy-start.18 = (f32[256,768]{1,0:T(8,128)S(1)}, f32[256,768]{1,0:T(8,128)}, u32[]{:S(2)}) copy-start(f32[256,768]{1,0:T(8,128)} %copy-done.17) | copy-start | bytes 2359300
  (51 other events, 352.6 us)
Sparse Core Ops, SparseCore 0:
  9.9 36.8 all-gather.5
  48.7 24.0 all-gather.7
  74.6 38.9 all-gather.9
  115.3 38.9 all-gather.11
  407.8 204.9 reduce-scatter.2
  618.6 134.5 reduce-scatter.4
  755.3 31.7 all-gather.13
where the time goes:
time: 815 us; the launch traced here: 806 us
  waiting for transfers between devices  370 us (45%)
  matrix products  194 us (24%)
  local copies, waits for them, and re-layouts  104 us (13%)
  blocking collectives  68.1 us (8%)
  starting transfers between devices  31.3 us (4%)
  other arithmetic  21.6 us (3%)
  between operations  16.7 us (2%)
    reduce_scatter x2, waiting for transfers between devices, on_device(): lax.psum_scatter(jnp.concatenate(pieces, axis=0), ('seq', 'dp'), scatter_...  266 us
    dot_general x128, matrix products, matmul_left_t(): lax.dot_general(left, right, (((0,), (0,)), ((), ())), preferred_element_...  127 us
    unnamed x192, local copies, waits for them, and re-layouts  40 us
    unnamed x2, blocking collectives  38.4 us
    concatenate x32, local copies, waits for them, and re-layouts, term_block(): return jnp.concatenate(pieces, axis=1)  36 us
    all_gather x1, blocking collectives, on_device(): lax.all_gather(hidden_block.astype(jnp.bfloat16), 'seq', axis=1, tiled=True)  18.9 us
    dot_general x4, matrix products, matmul(): return jnp.dot(left, right, preferred_element_type=jnp.float32)  16.7 us
  transfers between devices with their start and end apart: 15, of which 13 were waited for; matrix products, arithmetic and copies ran while one was open for 14% of the time, Pallas kernels for 0%

commit v1 on v0

v1 whole, which is shorter than its diff:
```python
import jax
import jax.numpy as jnp
from jax import lax
from jax.sharding import PartitionSpec as P

HEAD_DIM = 64
LOW = jnp.bfloat16
F32 = jnp.float32


def layer_norm(values, gain, bias):
    average = jnp.mean(values, -1, keepdims=True)
    centred = values - average
    variance = jnp.mean(centred * centred, -1, keepdims=True)
    return centred * lax.rsqrt(variance + 1e-05) * gain + bias


def gelu_tanh(values):
    return jax.nn.gelu(values, approximate=True)


def matmul(left, right):
    return jnp.dot(left, right, preferred_element_type=F32)


def matmul_left_t(left, right):
    return lax.dot_general(left, right, (((0,), (0,)), ((), ())), preferred_element_type=F32)


def matmul_right_t(left, right):
    return lax.dot_general(left, right, (((1,), (1,)), ((), ())), preferred_element_type=F32)


def gather_seq(value):
    return lax.all_gather(value, "seq", axis=0, tiled=True)


def scatter_seq(value):
    return lax.psum_scatter(value.astype(LOW), "seq", scatter_dimension=0, tiled=True).astype(F32)


def attention_forward(queries, keys, values):
    length, local_width = queries.shape
    heads_here = local_width // HEAD_DIM
    block_rows = min(512, length)
    blocks = length // block_rows
    scale = HEAD_DIM ** (-0.5)
    outs, logs = [], []
    key_index = jnp.arange(length)
    for b in range(blocks):
        seen = (b + 1) * block_rows
        q = queries[b * block_rows : seen].reshape(block_rows, heads_here, HEAD_DIM)
        k = keys[:seen].reshape(seen, heads_here, HEAD_DIM)
        v = values[:seen].reshape(seen, heads_here, HEAD_DIM)
        raw = jnp.einsum("qhd,khd->hqk", q, k, preferred_element_type=F32)
        positions = b * block_rows + jnp.arange(block_rows)
        causal = key_index[None, :seen] <= positions[:, None]
        scores = jnp.where(causal[None], raw * scale, -1e30)
        largest = jnp.max(scores, -1, keepdims=True)
        expo = jnp.exp(scores - largest)
        total = jnp.sum(expo, -1, keepdims=True)
        probs = (expo / total).astype(LOW)
        context = jnp.einsum("hqk,khd->qhd", probs, v, preferred_element_type=F32)
        outs.append(context.astype(LOW).reshape(block_rows, local_width))
        logs.append(largest + jnp.log(total))
    return jnp.concatenate(outs, axis=0), logs


def attention_backward(queries, keys, values, grads, logs):
    length, local_width = queries.shape
    heads_here = local_width // HEAD_DIM
    block_rows = min(512, length)
    blocks = length // block_rows
    scale = HEAD_DIM ** (-0.5)
    key_index = jnp.arange(length)
    query_grads = []
    key_sum = jnp.zeros((length, heads_here, HEAD_DIM), F32)
    value_sum = jnp.zeros((length, heads_here, HEAD_DIM), F32)
    for b in range(blocks):
        seen = (b + 1) * block_rows
        q = queries[b * block_rows : seen].reshape(block_rows, heads_here, HEAD_DIM)
        g = grads[b * block_rows : seen].reshape(block_rows, heads_here, HEAD_DIM)
        k = keys[:seen].reshape(seen, heads_here, HEAD_DIM)
        v = values[:seen].reshape(seen, heads_here, HEAD_DIM)
        raw = jnp.einsum("qhd,khd->hqk", q, k, preferred_element_type=F32)
        positions = b * block_rows + jnp.arange(block_rows)
        causal = key_index[None, :seen] <= positions[:, None]
        scores = jnp.where(causal[None], raw * scale, -1e30)
        probs = jnp.exp(scores - logs[b])
        low_probs = probs.astype(LOW)
        value_term = jnp.einsum("hqk,qhd->khd", low_probs, g, preferred_element_type=F32)
        prob_grad = jnp.einsum("qhd,khd->hqk", g, v, preferred_element_type=F32)
        score_grad = (
            probs * (prob_grad - jnp.sum(probs * prob_grad, -1, keepdims=True))
        ).astype(LOW)
        query_grad = jnp.einsum("hqk,khd->qhd", score_grad, k, preferred_element_type=F32) * scale
        key_term = jnp.einsum("hqk,qhd->khd", score_grad, q, preferred_element_type=F32) * scale
        pad = ((0, length - seen), (0, 0), (0, 0))
        key_sum = key_sum + jnp.pad(key_term, pad)
        value_sum = value_sum + jnp.pad(value_term, pad)
        query_grads.append(query_grad.astype(LOW).reshape(block_rows, local_width))
    return (
        jnp.concatenate(query_grads, axis=0),
        key_sum.astype(LOW).reshape(length, local_width),
        value_sum.astype(LOW).reshape(length, local_width),
    )


def on_device(
    tokens,
    qkv_weight,
    proj_weight,
    hidden_weight,
    output_weight,
    first_gain,
    first_bias,
    second_gain,
    second_bias,
    cotangent,
):
    parts = lax.axis_size("seq")
    groups = lax.axis_size("dp")
    part = lax.axis_index("seq")
    inputs_low = tokens[0]
    rows, width = inputs_low.shape
    model_rows = qkv_weight.shape[0]
    local_width = width // parts
    hidden_rows = output_weight.shape[0] // parts
    hidden_here = hidden_rows * groups

    qkv_here = lax.dynamic_index_in_dim(
        qkv_weight.reshape(model_rows, 3, parts, local_width), part, 2, keepdims=False
    ).reshape(model_rows, 3 * local_width)
    hidden_cols = lax.dynamic_index_in_dim(
        hidden_weight.reshape(model_rows, groups, parts, hidden_rows), part, 2, keepdims=False
    ).reshape(model_rows, hidden_here)
    output_here = lax.dynamic_slice_in_dim(output_weight, part * hidden_rows, hidden_rows, 0)
    norms = jnp.stack([first_gain, first_bias, second_gain, second_bias], axis=0)
    norms = lax.all_gather(norms, "dp", axis=1, tiled=True).astype(F32)
    gain_one, bias_one, gain_two, bias_two = norms[0], norms[1], norms[2], norms[3]
    all_tokens = gather_seq(inputs_low)
    wide_qkv = lax.all_gather(qkv_here, "dp", axis=0, tiled=True)
    wide_proj = lax.all_gather(proj_weight, "dp", axis=0, tiled=True)
    wide_hidden = lax.all_gather(hidden_cols, "dp", axis=0, tiled=True)
    wide_output = lax.all_gather(output_here, "dp", axis=0, tiled=True)
    all_grads = gather_seq(cotangent[0])

    inputs = all_tokens.astype(F32)
    lowered_one = layer_norm(inputs, gain_one, bias_one).astype(LOW)
    projected = matmul(lowered_one, wide_qkv).astype(LOW)
    queries = projected[:, :local_width]
    keys = projected[:, local_width : 2 * local_width]
    values = projected[:, 2 * local_width :]
    context_here, logs = attention_forward(queries, keys, values)
    context = lax.all_gather(context_here, "seq", axis=1, tiled=True)
    middle = inputs + matmul(context, wide_proj)
    lowered_two = layer_norm(middle, gain_two, bias_two).astype(LOW)
    hidden_pre = matmul(lowered_two, wide_hidden)
    activated_float, gelu_pull = jax.vjp(gelu_tanh, hidden_pre)
    activated = activated_float.astype(LOW)

    act_grad = matmul_right_t(all_grads, wide_output)
    pre_grad = gelu_pull(act_grad)[0].astype(LOW)
    normed_two_grad = scatter_seq(matmul_right_t(pre_grad, wide_hidden))
    ffn_out = scatter_seq(matmul(activated, wide_output))
    middle_own = lax.dynamic_slice_in_dim(middle, part * rows, rows, 0)
    block_out = middle_own + ffn_out
    _, norm_pull_two = jax.vjp(layer_norm, middle_own, gain_two, bias_two)
    middle_part, gain_two_term, bias_two_term = norm_pull_two(normed_two_grad)
    middle_grad = cotangent[0].astype(F32) + middle_part
    attn_grad = gather_seq(middle_grad.astype(LOW))

    proj_here = lax.dynamic_slice_in_dim(wide_proj, part * local_width, local_width, 0)
    context_grad = matmul_right_t(attn_grad, proj_here).astype(LOW)
    query_grads, key_grads, value_grads = attention_backward(
        queries, keys, values, context_grad, logs
    )
    qkv_grad = jnp.concatenate([query_grads, key_grads, value_grads], axis=1)
    normed_one_grad = scatter_seq(matmul_right_t(qkv_grad, wide_qkv))
    _, norm_pull_one = jax.vjp(layer_norm, inputs_low.astype(F32), gain_one, bias_one)
    input_part, gain_one_term, bias_one_term = norm_pull_one(normed_one_grad)
    tokens_gradient = (middle_grad + input_part).astype(LOW)

    attn_cols = lax.dynamic_slice_in_dim(attn_grad, part * local_width, local_width, 1)
    output_term = matmul_left_t(activated, all_grads).astype(LOW)
    hidden_term = matmul_left_t(lowered_two, pre_grad).astype(LOW)
    proj_term = matmul_left_t(context, attn_cols).astype(LOW)
    qkv_term = matmul_left_t(lowered_one, qkv_grad).astype(LOW)
    first_terms = jnp.concatenate([output_term, hidden_term], axis=1)
    second_terms = jnp.concatenate([proj_term, qkv_term], axis=1)
    first_sum = lax.psum_scatter(first_terms, "dp", scatter_dimension=0, tiled=True)
    second_sum = lax.psum_scatter(second_terms, "dp", scatter_dimension=0, tiled=True)
    first_all = lax.all_gather(first_sum, "seq", axis=0)
    second_all = lax.all_gather(second_sum, "seq", axis=0)
    output_gradient = first_all[:, :, :width].reshape(parts * hidden_rows, width).astype(F32)
    hidden_gradient = (
        first_all[:, :, width:]
        .reshape(parts, model_rows, groups, hidden_rows)
        .transpose(1, 2, 0, 3)
        .reshape(model_rows, parts * hidden_here)
        .astype(F32)
    )
    proj_gradient = (
        second_all[:, :, :local_width].transpose(1, 0, 2).reshape(model_rows, width).astype(F32)
    )
    qkv_gradient = (
        second_all[:, :, local_width:]
        .reshape(parts, model_rows, 3, local_width)
        .transpose(1, 2, 0, 3)
        .reshape(model_rows, 3 * width)
        .astype(F32)
    )
    norm_terms = jnp.stack([gain_one_term, bias_one_term, gain_two_term, bias_two_term], axis=0)
    norm_sum = lax.psum(norm_terms, ("seq", "dp"))
    norm_own = lax.dynamic_slice_in_dim(
        norm_sum, lax.axis_index("dp") * first_gain.shape[0], first_gain.shape[0], 1
    )
    return (
        block_out.astype(LOW)[None],
        tokens_gradient[None],
        qkv_gradient,
        proj_gradient,
        hidden_gradient,
        output_gradient,
        norm_own[0],
        norm_own[1],
        norm_own[2],
        norm_own[3],
    )


def solution(mesh):
    placed = (
        P("dp", "seq", None),
        P("dp", None),
        P("dp", None),
        P("dp", None),
        P("dp", None),
        P("dp"),
        P("dp"),
        P("dp"),
        P("dp"),
        P("dp", "seq", None),
    )
    return jax.shard_map(
        on_device,
        mesh=mesh,
        in_specs=placed,
        out_specs=(
            P("dp", "seq", None),
            P("dp", "seq", None),
            P("dp", None),
            P("dp", None),
            P("dp", None),
            P("dp", None),
            P("dp"),
            P("dp"),
            P("dp"),
            P("dp"),
        ),
        check_vma=False,
    )
```

time: 815 us -> 509 us (0.62)
  matrix products: 194 us -> 48.4 us
  waiting for transfers between devices: 370 us -> 278 us
  local copies, waits for them, and re-layouts: 104 us -> 38.9 us
  starting transfers between devices: 31.3 us -> 1.16 us
  blocking collectives: 68.1 us -> 85.8 us
  other arithmetic: 21.6 us -> 32.6 us
    reduce_scatter x2 -> x5, waiting for transfers between devices: 266 us -> 97.5 us  [the longest x1 35.3 us: on_device(): lax.psum_scatter(first_terms, 'dp', scatter_dimension=0, tiled=True)]
    all_gather x5 -> x8, waiting for transfers between devices: 39.6 us -> 179 us  [the longest x3 92.4 us: gather_seq(): return lax.all_gather(value, 'seq', axis=0, tiled=True)]
    dot_general x128 -> x4, matrix products: 127 us -> 8.21 us  [matmul_left_t(): lax.dot_general(left, right, (((0,), (0,)), ((), ())), preferred_element_...]
    all_to_all x8 -> x0, waiting for transfers between devices: 61.7 us -> none  [the longest x1 11.2 us: on_device(): lax.all_to_all(queries, 'seq', split_axis=1, concat_axis=0, tiled=True)]
    unnamed x2 -> x0, blocking collectives: 38.4 us -> none
    concatenate x33 -> x0, local copies, waits for them, and re-layouts: 36.9 us -> none  [the longest x32 36 us: term_block(): return jnp.concatenate(pieces, axis=1)]
    psum x1, blocking collectives: 10.7 us -> 41.4 us  [on_device(): norm_sum = lax.psum(norm_terms, ('seq', 'dp'))]
    all_to_all x8 -> x0, starting transfers between devices: 30.6 us -> none  [the longest x1 4.77 us: on_device(): lax.all_to_all(context_grad, 'seq', split_axis=1, concat_axis=0, tiled=True)]
  transfers between devices with their start and end apart: 15 -> 13, of which waited for: 13 -> 12; matrix products, arithmetic and copies ran while one was open for 14% -> 20% of each run, Pallas kernels for 0% -> 0%
where the time goes in v1:
time: 509 us; the launch traced here: 500 us
  waiting for transfers between devices  278 us (55%)
  blocking collectives  85.8 us (17%)
  matrix products  48.4 us (10%)
  local copies, waits for them, and re-layouts  38.9 us (8%)
  other arithmetic  32.6 us (6%)
  between operations  15.3 us (3%)
    all_gather x3, waiting for transfers between devices, gather_seq(): return lax.all_gather(value, 'seq', axis=0, tiled=True)  92.4 us
    psum x1, blocking collectives, on_device(): norm_sum = lax.psum(norm_terms, ('seq', 'dp'))  41.4 us
    all_gather x1, waiting for transfers between devices, on_device(): context = lax.all_gather(context_here, 'seq', axis=1, tiled=True)  39.3 us
    reduce_scatter x1, waiting for transfers between devices, on_device(): lax.psum_scatter(first_terms, 'dp', scatter_dimension=0, tiled=True)  35.3 us
    reduce_scatter x3, waiting for transfers between devices, scatter_seq(): lax.psum_scatter(value.astype(LOW), 'seq', scatter_dimension=0, tiled=True)  33.9 us
    reduce_scatter x1, waiting for transfers between devices, on_device(): lax.psum_scatter(second_terms, 'dp', scatter_dimension=0, tiled=True)  28.3 us
    all_gather x1, blocking collectives, on_device(): second_all = lax.all_gather(second_sum, 'seq', axis=0)  22.2 us
    all_gather x1, waiting for transfers between devices, on_device(): wide_output = lax.all_gather(output_here, 'dp', axis=0, tiled=True)  21 us
  transfers between devices with their start and end apart: 13, of which 12 were waited for; matrix products, arithmetic and copies ran while one was open for 20% of the time, Pallas kernels for 0%

profile of v1, /device:TPU:0, one launch (start us, length us, event | category | flops | bytes accessed | tf_op | source)
XLA Modules:
  0.0 500.2 jit_solution(855848961846258834)
XLA Ops:
  7.2 2.0 copy.123
  10.8 10.3 %all-gather.4 = bf16[8,96,4]{1,2,0:T(4,128)(2,1)S(1)} all-gather(bf16[1,96,4]{1,2,0:T(4,128)(2,1)S(1)} %maximum_bitcast_fusion), channel_id=1, replica_groups=mesh['seq'=4,'dp'=8] {'dp'}, dimensions={0}, use_global_device_ids=true | all-gather | bytes 6912 | tf_op jit(solution)/shard_map/all_gather | solution.py:139
  22.4 1.6 reshape.258
  24.7 11.9 %all_gather.41 = bf16[768,576]{1,0:T(8,128)(2,1)} all-gather(bf16[96,576]{1,0:T(8,128)(2,1)S(1)} %copy.126), channel_id=1, replica_groups=mesh['seq'=4,'dp'=8] {'dp'}, dimensions={0}, use_global_device_ids=true | all-gather | bytes 995328 | tf_op jit(solution)/shard_map/all_gather | solution.py:142
  36.7 13.9 %all-gather.24.cloned.1.call-done = bf16[1,1024,768]{1,2,0:T(8,128)(2,1)} async-done(((bf16[1,256,768]{1,2,0:T(8,128)(2,1)}), bf16[1,1024,768]{1,2,0:T(8,128)(2,1)}) %all-gather.24.cloned.1.call-update) | async-done | bytes 1572880 | tf_op jit(solution)/shard_map/all_gather | solution.py:35
  50.6 1.8 convert_reduce_fusion
  52.5 1.9 fusion.6
  59.2 1.5 fusion
  61.7 1.7 fusion.55
  68.8 6.1 %all-gather.16.cloned.1.call-done = bf16[768,768]{1,0:T(8,128)(2,1)} async-done(((bf16[96,768]{1,0:T(8,128)(2,1)}), bf16[768,768]{1,0:T(8,128)(2,1)}) %all-gather.16.cloned.1.call-update) | async-done | bytes 1179664 | tf_op jit(solution)/shard_map/all_gather | solution.py:143
  74.8 39.3 %all-gather.14.cloned.1.call-done = bf16[1024,768]{0,1:T(8,128)(2,1)} async-done(((bf16[1024,192]{0,1:T(8,128)(2,1)}), bf16[1024,768]{0,1:T(8,128)(2,1)}) %all-gather.14.cloned.1.call-update) | async-done | bytes 1572880 | tf_op jit(solution)/shard_map/all_gather | solution.py:155
  114.1 3.7 fusion.90
  118.5 1.7 add_convert_fusion
  120.2 19.2 %all-gather.18.cloned.1.call-done = bf16[768,768]{1,0:T(8,128)(2,1)} async-done(((bf16[96,768]{1,0:T(8,128)(2,1)}), bf16[768,768]{1,0:T(8,128)(2,1)}) %all-gather.18.cloned.1.call-update) | async-done | bytes 1179664 | tf_op jit(solution)/shard_map/all_gather | solution.py:144
  139.4 4.8 fusion.91
  144.2 21.0 %all-gather.20.cloned.1.call-done = bf16[768,768]{1,0:T(8,128)(2,1)} async-done(((bf16[96,768]{1,0:T(8,128)(2,1)}), bf16[768,768]{1,0:T(8,128)(2,1)}) %all-gather.20.cloned.1.call-update) | async-done | bytes 1179664 | tf_op jit(solution)/shard_map/all_gather | solution.py:145
  165.2 38.5 %all-gather.26.cloned.1.call-done = bf16[1,1024,768]{2,1,0:T(8,128)(2,1)} async-done(((bf16[1,256,768]{2,1,0:T(8,128)(2,1)}), bf16[1,1024,768]{2,1,0:T(8,128)(2,1)}) %all-gather.26.cloned.1.call-update) | async-done | bytes 1572880 | tf_op jit(solution)/shard_map/all_gather | solution.py:35
  203.8 5.6 %fusion.16 = bf16[1024,768]{1,0:T(8,128)(2,1)S(1)} fusion(f32[1024,768]{1,0:T(8,128)} %fusion.91, bf16[768,768]{1,0:T(8,128)(2,1)} %all-gather.20.cloned.1.call-done, bf16[1,1024,768]{2,1,0:T(8,128)(2,1)} %all-gather.26.cloned.1.call-done), kind=kOutput, calls=%fused_computation.26 | convolution fusion | flops 1223688192 | bytes 7471104 | tf_op jit(solution)/shard_map/dot_general | solution.py:31
  210.5 2.6 convolution_convert_fusion.1
  213.5 3.5 convolution_convert_fusion.3
  217.0 1.7 fusion.33
  218.7 1.5 pad_maximum_fusion
  220.2 4.3 copy.156
  224.6 1.9 copy.130
  227.2 20.3 %reduce-scatter.12.cloned.1.call-done = bf16[256,768]{0,1:T(8,128)(2,1)} async-done(((bf16[1024,768]{0,1:T(8,128)(2,1)}), bf16[256,768]{0,1:T(8,128)(2,1)}) %reduce-scatter.12.cloned.1.call-update) | async-done | bytes 393232 | tf_op jit(solution)/shard_map/reduce_scatter | solution.py:39
  247.5 2.0 multiply_reduce_fusion.3
  249.5 2.1 fusion.67
  252.2 2.7 fusion.70
  257.0 35.3 %reduce-scatter.18.cloned.1.call-done = bf16[96,1536]{1,0:T(8,128)(2,1)} async-done(((bf16[768,1536]{1,0:T(8,128)(2,1)}), bf16[96,1536]{1,0:T(8,128)(2,1)}) %reduce-scatter.18.cloned.1.call-update) | async-done | bytes 294928 | tf_op jit(solution)/shard_map/reduce_scatter | solution.py:191
  292.4 39.9 %all-gather.22.cloned.1.call-done = bf16[1024,768]{0,1:T(8,128)(2,1)} async-done(((bf16[256,768]{0,1:T(8,128)(2,1)}), bf16[1024,768]{0,1:T(8,128)(2,1)}) %all-gather.22.cloned.1.call-update) | async-done | bytes 1572880 | tf_op jit(solution)/shard_map/all_gather | solution.py:35
  332.3 2.0 convolution_convert_fusion.6
  334.4 1.5 multiply_reduce_fusion.1
  339.3 1.9 multiply_reduce_fusion
  344.0 1.7 convolution_convert_fusion.7
  351.5 2.5 convolution_convert_fusion
  354.4 5.0 %convolution_convert_fusion.2 = bf16[1024,768]{0,1:T(8,128)(2,1)} fusion(bf16[768,768]{1,0:T(8,128)(2,1)} %all-gather.20.cloned.1.call-done, f32[1024,768]{1,0:T(8,128)} %fusion.91), kind=kOutput, calls=%fused_computation.50 | convolution fusion | flops 1215823872 | bytes 5898240 | tf_op jit(solution)/shard_map/dot_general | solution.py:23
  362.5 2.4 fusion.84
  364.9 1.9 reshape.285
  366.9 2.2 copy.143
  369.0 3.6 reshape.282
  373.8 28.3 %reduce-scatter.16.cloned.1.call-done = bf16[96,768]{1,0:T(8,128)(2,1)} async-done(((bf16[768,768]{1,0:T(8,128)(2,1)}), bf16[96,768]{1,0:T(8,128)(2,1)}) %reduce-scatter.16.cloned.1.call-update) | async-done | bytes 147472 | tf_op jit(solution)/shard_map/reduce_scatter | solution.py:192
  402.1 22.2 %all-gather.2 = bf16[384,768]{1,0:T(8,128)(2,1)S(1)} all-gather(bf16[96,768]{1,0:T(8,128)(2,1)} %reduce-scatter.16.cloned.1.call-done), channel_id=4, replica_groups=mesh['seq'=4,'dp'=8] {'seq'}, dimensions={0}, use_global_device_ids=true | all-gather | bytes 737280 | tf_op jit(solution)/shard_map/all_gather | solution.py:194
  426.2 1.5 copy.140
  427.8 2.9 reshape.280
  430.7 13.6 %reduce-scatter.14.cloned.1.call-done = bf16[256,768]{0,1:T(8,128)(2,1)} async-done(((bf16[1024,768]{0,1:T(8,128)(2,1)}), bf16[256,768]{0,1:T(8,128)(2,1)}) %reduce-scatter.14.cloned.1.call-update) | async-done | bytes 393232 | tf_op jit(solution)/shard_map/reduce_scatter | solution.py:39
  445.8 1.5 fusion.68
  447.3 41.4 %psum.7 = f32[4,768]{1,0:T(4,128)S(1)} all-reduce(f32[4,768]{1,0:T(4,128)S(1)} %pad_maximum_fusion.6), channel_id=1, replica_groups=mesh['seq'=4,'dp'=8] {'seq','dp'}, use_global_device_ids=true, to_apply=%region_27.28 | all-reduce | flops 3072 | bytes 24576 | tf_op jit(solution)/shard_map/psum | solution.py:214
  489.4 2.0 fusion.73
  (212 shorter events, 42.2 us)
Async XLA Ops:
  7.2 60.2 %copy-start = (bf16[384,768]{1,0:T(8,128)(2,1)S(1)}, bf16[384,768]{1,0:T(8,128)(2,1)}, u32[]{:S(2)}) copy-start(bf16[384,768]{1,0:T(8,128)(2,1)} %param.14) | copy-start | bytes 1769476
  7.2 43.4 %all-gather.24.cloned.1.call-start = ((), (), s32[]{:S(2)}) async-start(), calls=%async_computation.13 | async-start | bytes 1966080 | tf_op jit(solution)/shard_map/all_gather | solution.py:35
  9.2 65.6 %all-gather.16.cloned.1.call-start = ((), (), s32[]{:S(2)}) async-start(), calls=%async_computation.6 | async-start | bytes 1327104 | tf_op jit(solution)/shard_map/all_gather | solution.py:143
  10.0 104.1 %all-gather.14.cloned.1.call-start = ((), (), s32[]{:S(2)}) async-start(), calls=%async_computation.5 | async-start | bytes 1966080 | tf_op jit(solution)/shard_map/all_gather | solution.py:155
  21.8 32.5 %copy-start.47 = (f32[768]{0:T(1024)}, f32[768]{0:T(1024)S(1)}, u32[]{:S(2)}) copy-start(f32[768]{0:T(1024)S(1)} %get-tuple-element.82) | copy-start | bytes 9220
  50.6 4.3 copy-start.7
  50.6 4.3 copy-start.19
  52.4 3.8 copy-start.36
  56.3 2.3 copy-start.11
  56.4 4.3 copy-start.21
  56.4 5.2 %copy-start.17 = (bf16[1024,192]{0,1:T(8,128)(2,1)}, bf16[1024,192]{0,1:T(8,128)(2,1)S(1)}, u32[]{:S(2)}) copy-start(bf16[1024,192]{0,1:T(8,128)(2,1)S(1)} %get-tuple-element.93) | copy-start | bytes 1179652
  57.2 3.5 copy-start.3
  58.7 3.0 copy-start.2
  58.7 3.0 copy-start.29
  61.7 2.7 copy-start.23
  64.2 75.2 %all-gather.18.cloned.1.call-start = ((), (), s32[]{:S(2)}) async-start(), calls=%async_computation.7 | async-start | bytes 1327104 | tf_op jit(solution)/shard_map/all_gather | solution.py:144
  67.3 97.9 %all-gather.20.cloned.1.call-start = ((), (), s32[]{:S(2)}) async-start(), calls=%async_computation.8 | async-start | bytes 1327104 | tf_op jit(solution)/shard_map/all_gather | solution.py:145
  68.1 135.6 %all-gather.26.cloned.1.call-start = ((), (), s32[]{:S(2)}) async-start(), calls=%async_computation.14 | async-start | bytes 1966080 | tf_op jit(solution)/shard_map/all_gather | solution.py:35
  68.7 178.8 %reduce-scatter.12.cloned.1.call-start = ((), (), s32[]{:S(2)}) async-start(), calls=%async_computation.10 | async-start | bytes 1966080 | tf_op jit(solution)/shard_map/reduce_scatter | solution.py:39
  117.8 131.7 %copy-start.5 = (f32[1024,768]{0,1:T(8,128)}, f32[1024,768]{0,1:T(8,128)S(1)}, u32[]{:S(2)}) copy-start(f32[1024,768]{0,1:T(8,128)S(1)} %get-tuple-element.109) | copy-start | bytes 9437188
  203.8 6.8 %copy-start.53 = (bf16[768,768]{1,0:T(8,128)(2,1)S(1)}, bf16[768,768]{1,0:T(8,128)(2,1)}, u32[]{:S(2)}) copy-start(bf16[768,768]{1,0:T(8,128)(2,1)} %all-gather.18.cloned.1.call-done) | copy-start | bytes 3538948
  213.2 79.2 %reduce-scatter.18.cloned.1.call-start = ((), (), s32[]{:S(2)}) async-start(), calls=%async_computation.17 | async-start | bytes 2654208 | tf_op jit(solution)/shard_map/reduce_scatter | solution.py:191
  213.4 3.5 copy-start.52
  213.5 3.5 copy-start.54
  224.5 107.7 %all-gather.22.cloned.1.call-start = ((), (), s32[]{:S(2)}) async-start(), calls=%async_computation.11 | async-start | bytes 1966080 | tf_op jit(solution)/shard_map/all_gather | solution.py:35
  251.6 82.8 %copy-start.4 = (f32[3,512,512]{1,2,0:T(8,128)S(1)}, f32[3,512,512]{1,2,0:T(8,128)}, u32[]{:S(2)}) copy-start(f32[3,512,512]{1,2,0:T(8,128)} %copy-done.3) | copy-start | bytes 9437188
  255.0 107.6 %all-gather.28.cloned.1.call-start = ((), (), s32[]{:S(2)}) async-start(), calls=%async_computation.15 | async-start | bytes 1474560 | tf_op jit(solution)/shard_map/all_gather | solution.py:193
  292.4 109.7 %reduce-scatter.16.cloned.1.call-start = ((), (), s32[]{:S(2)}) async-start(), calls=%async_computation.16 | async-start | bytes 1327104 | tf_op jit(solution)/shard_map/reduce_scatter | solution.py:192
  335.9 2.4 slice-start
  335.9 3.1 slice-start.1
  337.4 10.9 %copy-start.26 = (bf16[3,64,512]{2,1,0:T(8,128)(2,1)}, bf16[3,64,512]{2,1,0:T(8,128)(2,1)S(1)}, u32[]{:S(2)}) copy-start(bf16[3,64,512]{2,1,0:T(8,128)(2,1)S(1)} %fusion.52) | copy-start | bytes 589828
  342.6 3.2 copy-start.12
  344.0 4.3 copy-start.24
  351.4 92.9 %reduce-scatter.14.cloned.1.call-start = ((), (), s32[]{:S(2)}) async-start(), calls=%async_computation.12 | async-start | bytes 1966080 | tf_op jit(solution)/shard_map/reduce_scatter | solution.py:39
  354.1 5.4 %copy-start.6 = (bf16[1,256,768]{1,2,0:T(8,128)(2,1)S(1)}, bf16[1,256,768]{1,2,0:T(8,128)(2,1)}, u32[]{:S(2)}) copy-start(bf16[1,256,768]{1,2,0:T(8,128)(2,1)} %copy.123) | copy-start | bytes 1179652
  354.1 6.1 %copy-start.34 = (f32[768]{0:T(1024)S(1)}, f32[768]{0:T(1024)}, u32[]{:S(2)}) copy-start(f32[768]{0:T(1024)} %get-tuple-element.79) | copy-start | bytes 9220
  354.1 6.7 %copy-start.35 = (f32[768]{0:T(1024)S(1)}, f32[768]{0:T(1024)}, u32[]{:S(2)}) copy-start(f32[768]{0:T(1024)} %get-tuple-element.70) | copy-start | bytes 9220
  354.1 135.2 %reduce-scatter.10.cloned.1.call-start = ((), (), s32[]{:S(2)}) async-start(), calls=%async_computation.9 | async-start | bytes 1966080 | tf_op jit(solution)/shard_map/reduce_scatter | solution.py:39
  426.1 18.2 %copy-start.38 = (f32[256]{0:T(256)S(1)}, f32[256]{0:T(256)}, u32[]{:S(2)}) copy-start(f32[256]{0:T(256)} %broadcast_multiply_fusion.2) | copy-start | bytes 3076
  426.1 21.2 %copy-start.43 = (f32[1,768]{1,0:T(1,128)S(1)}, f32[1,768]{1,0:T(1,128)}, u32[]{:S(2)}) copy-start(f32[1,768]{1,0:T(1,128)} %reshape.279) | copy-start | bytes 9220
  426.1 21.2 %copy-start.44 = (f32[1,768]{1,0:T(1,128)S(1)}, f32[1,768]{1,0:T(1,128)}, u32[]{:S(2)}) copy-start(f32[1,768]{1,0:T(1,128)} %reshape.278) | copy-start | bytes 9220
  426.2 63.2 %copy-start.9 = (bf16[256,768]{0,1:T(8,128)(2,1)S(1)}, bf16[256,768]{0,1:T(8,128)(2,1)}, u32[]{:S(2)}) copy-start(bf16[256,768]{0,1:T(8,128)(2,1)} %reduce-scatter.12.cloned.1.call-done) | copy-start | bytes 1179652
  426.2 63.1 %copy-start.10 = (bf16[1,256,768]{1,2,0:T(8,128)(2,1)S(1)}, bf16[1,256,768]{1,2,0:T(8,128)(2,1)}, u32[]{:S(2)}) copy-start(bf16[1,256,768]{1,2,0:T(8,128)(2,1)} %copy.130) | copy-start | bytes 1179652
  426.2 63.1 %copy-start.32 = (f32[256]{0:T(256)S(1)}, f32[256]{0:T(256)}, u32[]{:S(2)}) copy-start(f32[256]{0:T(256)} %broadcast_multiply_fusion.3) | copy-start | bytes 3076
  426.2 63.1 %copy-start.40 = (f32[256]{0:T(256)S(1)}, f32[256]{0:T(256)}, u32[]{:S(2)}) copy-start(f32[256]{0:T(256)} %copy-done.39) | copy-start | bytes 3076
  426.2 63.1 %copy-start.42 = (f32[256]{0:T(256)S(1)}, f32[256]{0:T(256)}, u32[]{:S(2)}) copy-start(f32[256]{0:T(256)} %copy-done.41) | copy-start | bytes 3076
  426.2 63.1 %copy-start.46 = (f32[256]{0:T(256)S(1)}, f32[256]{0:T(256)}, u32[]{:S(2)}) copy-start(f32[256]{0:T(256)} %copy-done.45) | copy-start | bytes 3076
  444.3 48.9 %copy-start.1 = (bf16[384,768]{1,0:T(8,128)(2,1)S(1)}, bf16[384,768]{1,0:T(8,128)(2,1)}, u32[]{:S(2)}) copy-start(bf16[384,768]{1,0:T(8,128)(2,1)} %param.14) | copy-start | bytes 1769476
  (23 other events, 35.3 us)
Sparse Core Ops, SparseCore 0:
  10.2 40.3 all-gather.23
  52.5 22.3 all-gather.15
  77.0 37.0 all-gather.13
  116.4 22.9 all-gather.17
  141.1 24.0 all-gather.19
  166.6 37.0 all-gather.25
  213.3 34.1 reduce-scatter.11
  250.9 41.4 reduce-scatter.17
  294.6 37.6 all-gather.21
  333.8 28.7 all-gather.27
  366.1 35.8 reduce-scatter.15
  404.2 40.0 reduce-scatter.13
  446.6 35.2 reduce-scatter.9
